TPU v7x, 32 devices: a whole 2x2x4 slice. The times are simulated.
32 devices in a mesh: dp: 8 (over y, x, core), seq: 4 (over z).
Axes of the slice: x: 2, y: 2, z: 4, core: 2. Of those that a mesh axis runs over, the one named last changes fastest.
Arguments:
- grad_out: bfloat16 [4096, 1280], P(('dp', 'seq')), may hold values from -6 to 6
- saved_input: bfloat16 [4096, 1280], P(('dp', 'seq')), may hold values from -6 to 6
- pre_glu: bfloat16 [4096, 2560], P(('dp', 'seq')), may hold values from -6 to 6
- queries: bfloat16 [4096, 1280], P('dp', 'seq'), may hold values from -8 to 8
- keys: bfloat16 [4096, 1280], P('dp', 'seq'), may hold values from -8 to 8
- values: bfloat16 [4096, 1280], P('dp', 'seq'), may hold values from -6 to 6
- frame_counts: int32 [8, 8], P('dp'), may hold values from 1 to 256, 512 in all within a row
- norm_gain: float32 [1280], replicated, may hold values from 0.5 to 1.5
- kernel: float32 [31, 1280], replicated, may hold values from -1 to 1
- w_in: bfloat16 [1280, 2560], P('dp'), may hold values from -0.15625 to 0.15625
- w_conv_out: bfloat16 [1280, 1280], P('dp'), may hold values from -0.15625 to 0.15625
- w_attn_out: bfloat16 [1280, 1280], P('dp'), may hold values from -0.15625 to 0.15625
Outputs:
- resid_grad: bfloat16 [4096, 1280], P(('dp', 'seq'))
- query_grad: bfloat16 [4096, 1280], P('dp', 'seq')
- key_grad: bfloat16 [4096, 1280], P('dp', 'seq')
- value_grad: bfloat16 [4096, 1280], P('dp', 'seq')
- kernel_grad: float32 [31, 1280], replicated
- gain_grad: float32 [1280], replicated
Inputs may be any that keep to these rules, and one draw needn't show every extreme that they name: `frame_counts`: each row sums to 512; its largest entry is exactly 256.
All inputs are finite; a program needn't handle non-finite values.
Results may differ from a plain program's by a relative error of at most 0.018.
Values may be sent and summed in bfloat16 or wider, within the bound.
A program may use at most 64 MiB of HBM per device.

v0:
```python
import math

import jax
import jax.numpy as jnp
from jax import lax
from jax.sharding import PartitionSpec as P

HD = 80
KW = 31


def padded(block, sides, width):
    for axis, dim in sides:
        count = lax.axis_size(axis)
        forward = [(i, i + 1) for i in range(count - 1)]
        backward = [(target, source) for source, target in forward]
        low = lax.ppermute(
            lax.slice_in_dim(block, block.shape[dim] - width, None, axis=dim), axis, forward
        )
        high = lax.ppermute(lax.slice_in_dim(block, 0, width, axis=dim), axis, backward)
        block = jnp.concatenate([low, block, high], axis=dim)
    return block


def segments_of(frame_lens, positions):
    ends = jnp.cumsum(frame_lens)
    counted = jnp.sum((positions[:, None] >= ends[None, :]).astype(jnp.int32), axis=1)
    return jnp.where(positions < 0, jnp.int32(-1), counted)


def row_product(active, piece):
    return jnp.einsum("tc,rc->tr", active, piece, preferred_element_type=jnp.float32)


def attention_backward(query_rows, key_rows, value_rows, out_grad, seg_all):
    total, columns = query_rows.shape
    heads = columns // HD
    scale = 1.0 / math.sqrt(HD)
    query_heads = query_rows.reshape(total, heads, HD)
    key_heads = key_rows.reshape(total, heads, HD)
    value_heads = value_rows.reshape(total, heads, HD)
    grad_heads = out_grad.reshape(total, heads, HD)
    qblock = min(512, total)
    nblocks = total // qblock

    def block_step(block, carry):
        query_out, key_acc, value_acc = carry
        qstart = block * qblock
        query_block = lax.dynamic_slice_in_dim(query_heads, qstart, qblock, 0)
        grad_block = lax.dynamic_slice_in_dim(grad_heads, qstart, qblock, 0)
        seg_query = lax.dynamic_slice_in_dim(seg_all, qstart, qblock, 0)
        scores = (
            jnp.einsum("qhd,khd->hqk", query_block, key_heads, preferred_element_type=jnp.float32)
            * scale
        )
        scores = jnp.where((seg_query[:, None] == seg_all[None, :])[None], scores, -1e30)
        peak = jnp.max(scores, axis=2, keepdims=True)
        expd = jnp.exp(scores - peak)
        probs = expd / jnp.sum(expd, axis=2, keepdims=True)
        probs_low = probs.astype(jnp.bfloat16)
        value_part = jnp.einsum(
            "hqk,qhd->khd", probs_low, grad_block, preferred_element_type=jnp.float32
        )
        prob_grad = jnp.einsum(
            "qhd,khd->hqk", grad_block, value_heads, preferred_element_type=jnp.float32
        )
        delta = jnp.sum(probs * prob_grad, axis=2, keepdims=True)
        score_grad = (probs * (prob_grad - delta)).astype(jnp.bfloat16)
        query_part = (
            jnp.einsum("hqk,khd->qhd", score_grad, key_heads, preferred_element_type=jnp.float32)
            * scale
        ).astype(jnp.bfloat16)
        key_part = jnp.einsum(
            "hqk,qhd->khd", score_grad, query_block, preferred_element_type=jnp.float32
        )
        query_out = lax.dynamic_update_slice_in_dim(query_out, query_part, qstart, 0)
        return (query_out, key_acc + key_part, value_acc + value_part)

    initial = (
        jnp.zeros((total, heads, HD), jnp.bfloat16),
        jnp.zeros((total, heads, HD), jnp.float32),
        jnp.zeros((total, heads, HD), jnp.float32),
    )
    query_out, key_acc, value_acc = lax.fori_loop(0, nblocks, block_step, initial)
    key_grad = (key_acc * scale).astype(jnp.bfloat16)
    value_grad = value_acc.astype(jnp.bfloat16)
    return (
        query_out.reshape(total, columns),
        key_grad.reshape(total, columns),
        value_grad.reshape(total, columns),
    )


def local(
    grad_out,
    saved_input,
    pre_glu,
    queries,
    keys,
    values,
    frame_counts,
    norm_gain,
    kernel,
    w_in,
    w_conv_out,
    w_attn_out,
):
    t_dev, width = grad_out.shape
    n_seq = lax.axis_size("seq")
    total = t_dev * n_seq
    half = KW // 2
    frame_lens = frame_counts[0]
    seq_index = lax.axis_index("seq")
    ext_pos = seq_index * t_dev + jnp.arange(-half, t_dev + half, dtype=jnp.int32)
    seg_ext = segments_of(frame_lens, ext_pos)
    seg_own = seg_ext[half : half + t_dev]
    first_half = pre_glu[:, :width].astype(jnp.float32)
    gate_sig = jax.nn.sigmoid(pre_glu[:, width:].astype(jnp.float32))
    glu_out = (first_half * gate_sig).astype(jnp.bfloat16)
    glu_ext = padded(glu_out, (("seq", 0),), half).astype(jnp.float32)
    matches = [
        (seg_ext[tap_index : tap_index + t_dev] == seg_own).astype(jnp.float32)[:, None]
        for tap_index in range(KW)
    ]
    conv_out = jnp.zeros((t_dev, width), jnp.float32)
    for tap_index in range(KW):
        conv_out = (
            conv_out
            + kernel[tap_index] * glu_ext[tap_index : tap_index + t_dev] * matches[tap_index]
        )
    conv_out_grad = row_product(grad_out, lax.all_gather(w_conv_out, "dp", axis=0, tiled=True))
    conv_sig = jax.nn.sigmoid(conv_out)
    conv_grad = (conv_out_grad * conv_sig * (1.0 + conv_out * (1.0 - conv_sig))).astype(
        jnp.bfloat16
    )
    grad_ext = padded(conv_grad, (("seq", 0),), half).astype(jnp.float32)
    grad_float = grad_ext[half : half + t_dev]
    glu_grad = jnp.zeros((t_dev, width), jnp.float32)
    kernel_rows = []
    for tap_index in range(KW):
        back = 2 * half - tap_index
        glu_grad = glu_grad + kernel[tap_index] * grad_ext[back : back + t_dev] * matches[back]
        kernel_rows.append(
            jnp.sum(
                grad_float * glu_ext[tap_index : tap_index + t_dev] * matches[tap_index], axis=0
            )
        )
    glu_in_grad = jnp.concatenate(
        [glu_grad * gate_sig, glu_grad * first_half * gate_sig * (1.0 - gate_sig)], axis=1
    ).astype(jnp.bfloat16)
    norm_grad = row_product(glu_in_grad, lax.all_gather(w_in, "dp", axis=0, tiled=True))
    inputs = saved_input.astype(jnp.float32)
    centred = inputs - jnp.mean(inputs, axis=1, keepdims=True)
    inv_std = 1.0 / jnp.sqrt(jnp.mean(centred * centred, axis=1, keepdims=True) + 1e-05)
    normed = centred * inv_std
    scaled_grad = norm_grad * norm_gain
    input_grad = inv_std * (
        scaled_grad
        - jnp.mean(scaled_grad, axis=1, keepdims=True)
        - normed * jnp.mean(scaled_grad * normed, axis=1, keepdims=True)
    )
    resid_grad = (grad_out.astype(jnp.float32) + input_grad).astype(jnp.bfloat16)
    gain_term = jnp.sum(norm_grad * normed, axis=0)
    ctx_float = row_product(resid_grad, lax.all_gather(w_attn_out, "dp", axis=0, tiled=True))
    ctx_grad = ctx_float.astype(jnp.bfloat16)
    relayed = lax.all_to_all(ctx_grad, "seq", split_axis=1, concat_axis=0, tiled=True)
    seg_all = segments_of(frame_lens, jnp.arange(total, dtype=jnp.int32))
    query_grad, key_grad, value_grad = attention_backward(queries, keys, values, relayed, seg_all)
    kernel_grad, gain_grad = lax.psum((jnp.stack(kernel_rows), gain_term), ("dp", "seq"))
    return (resid_grad, query_grad, key_grad, value_grad, kernel_grad, gain_grad)


def solution(mesh):
    in_specs = (
        P(("dp", "seq"), None),
        P(("dp", "seq"), None),
        P(("dp", "seq"), None),
        P("dp", "seq"),
        P("dp", "seq"),
        P("dp", "seq"),
        P("dp", None),
        P(),
        P(),
        P("dp", None),
        P("dp", None),
        P("dp", None),
    )
    out_specs = (P(("dp", "seq"), None), P("dp", "seq"), P("dp", "seq"), P("dp", "seq"), P(), P())
    return jax.shard_map(local, mesh=mesh, in_specs=in_specs, out_specs=out_specs, check_vma=False)
```

profile of v0, /device:TPU:0, one launch (start us, length us, event | category | flops | bytes accessed | tf_op | source)
XLA Modules:
  0.0 274.7 jit_solution(8329521554390509209)
XLA Ops:
  7.2 0.7 all-gather.4.cloned.1.call-update
  8.0 0.7 all-gather.6.cloned.1.call-update
  8.7 1.3 fusion.26
  10.0 4.9 %collective-permute-start = (bf16[15,1280]{1,0:T(8,128)(2,1)S(1)}, bf16[15,1280]{1,0:T(8,128)(2,1)S(1)}, u32[]{:S(2)}, u32[]{:S(2)}) collective-permute-start(bf16[15,1280]{1,0:T(8,128)(2,1)S(1)} %get-tuple-element.105), channel_id=1, source_target_pairs={{0,1},{1,2},{2,3},{4,5},{5,6},{6,7},{8,9},{9,10},{10,11},{12,13},{... | collective-permute-start | bytes 115208 | tf_op jit(solution)/shard_map/ppermute | solution.py:17
  14.9 1.3 collective-permute-start.1
  16.3 0.8 reduce-window.8
  17.1 0.1 convert_reduce_fusion.2
  17.4 0.1 compare_convert_fusion.26
  17.5 0.1 convert_reduce_fusion.1
  17.6 1.6 slice_reduce_fusion.30
  19.2 1.1 convert_reduce_fusion
  20.3 1.3 fusion.25
  21.6 0.2 broadcast_compare_fusion
  21.8 4.8 %fusion.102 = (f32[4,512]{1,0:T(4,128)S(1)}, f32[4,512,512]{1,2,0:T(8,128)}) fusion(pred[512,512]{0,1:T(8,128)(4,1)S(1)} %broadcast_compare_fusion, bf16[512,4,80]{0,2,1:T(8,128)(2,1)S(1)} %bitcast.34, bf16[512,4,80]{0,2,1:T(8,128)(2,1)} %bitcast.37), kind=kOutput, calls=%fused_computation.248 | convolution fusion | flops 171966976 | bytes 5120000 | tf_op jit(solution)/shard_map/while/body/eval_jaxpr/sub | solution.py:58
  26.6 1.3 slice_reduce_fusion.29
  28.0 0.1 maximum_convert_fusion
  28.1 17.4 %all-gather.4.cloned.1.call-done = bf16[1280,1280]{1,0:T(8,128)(2,1)} async-done(((bf16[160,1280]{1,0:T(8,128)(2,1)}), bf16[1280,1280]{1,0:T(8,128)(2,1)}) %all-gather.4.cloned.1.call-update) | async-done | bytes 3276816 | tf_op jit(solution)/shard_map/all_gather | solution.py:131
  45.5 5.6 %fusion.3 = bf16[128,1280]{1,0:T(8,128)(2,1)S(1)} fusion(bf16[128,1280]{1,0:T(8,128)(2,1)S(1)} %copy-done.5, bf16[1280,1280]{1,0:T(8,128)(2,1)} %all-gather.4.cloned.1.call-done, f32[158,1280]{1,0:T(8,128)S(1)} %maximum_convert_fusion, f32[128]{0:T(128)S(1)} %get-tuple-element.135, f32[1280]{0:T(1024)S(1)} %get-tuple-element.98, ...), kind=kOutput, calls=%fused_computation.8 | convolution fusion | flops 435814400 | bytes 24422400 | tf_op jit(solution)/shard_map/tc,rc->tr/dot_general | solution.py:32
  51.1 3.4 %collective-permute-start.2 = (bf16[15,1280]{1,0:T(8,128)(2,1)S(1)}, bf16[15,1280]{1,0:T(8,128)(2,1)S(1)}, u32[]{:S(2)}, u32[]{:S(2)}) collective-permute-start(bf16[15,1280]{1,0:T(8,128)(2,1)S(1)} %get-tuple-element.103), channel_id=1, source_target_pairs={{0,1},{1,2},{2,3},{4,5},{5,6},{6,7},{8,9},{9,10},{10,11},{12,13},{... | collective-permute-start | bytes 115208 | tf_op jit(solution)/shard_map/ppermute | solution.py:17
  54.5 1.5 collective-permute-start.3
  56.0 0.2 collective-permute-done.2
  56.2 4.2 %collective-permute-done.3 = bf16[15,1280]{1,0:T(8,128)(2,1)S(1)} collective-permute-done((bf16[15,1280]{1,0:T(8,128)(2,1)S(1)}, bf16[15,1280]{1,0:T(8,128)(2,1)S(1)}, u32[]{:S(2)}, u32[]{:S(2)}) %collective-permute-start.3) | collective-permute-done | bytes 38432 | tf_op jit(solution)/shard_map/ppermute | solution.py:20
  60.4 0.1 maximum_convert_fusion.1
  60.5 0.9 multiply_reduce_fusion.25
  61.4 0.8 multiply_reduce_fusion.7
  62.2 0.9 multiply_reduce_fusion.1
  63.1 3.9 %multiply_convert_fusion.1 = (bf16[128,1280]{1,0:T(8,128)(2,1)S(1)}, f32[128,1280]{1,0:T(8,128)S(1)}) fusion(bf16[128,2560]{1,0:T(8,128)(2,1)S(1)} %copy-done.2, f32[128]{0:T(128)S(1)} %get-tuple-element.136, f32[158,1280]{1,0:T(8,128)S(1)} %maximum_convert_fusion.1, f32[1280]{0:T(1024)S(1)} %get-tuple-element.98, f32[128]{0:T(128)S(1)} %get-tuple-element.107, ...), kind=kLoop, calls=%fused_computation.166 | loop fusion | flops 15892480 | bytes 21800960 | tf_op jit(solution)/shard_map/convert
  67.0 0.2 fusion.29
  67.3 26.8 %all-gather.6.cloned.1.call-done = bf16[1280,2560]{1,0:T(8,128)(2,1)} async-done(((bf16[160,2560]{1,0:T(8,128)(2,1)}), bf16[1280,2560]{1,0:T(8,128)(2,1)}) %all-gather.6.cloned.1.call-update) | async-done | bytes 6553616 | tf_op jit(solution)/shard_map/all_gather | solution.py:151
  94.1 5.2 %fusion.24 = (f32[1280]{0:T(1024)S(1)}, f32[128]{0:T(128)S(1)}, f32[128]{0:T(128)S(1)}, f32[128,1280]{1,0:T(8,128)S(1)}) fusion(bf16[128,1280]{1,0:T(8,128)(2,1)S(1)} %copy-done.3, f32[128]{0:T(128)S(1)} %add_rsqrt_fusion, f32[128]{0:T(128)S(1)} %broadcast_multiply_fusion.2, f32[1280]{0:T(1024)S(1)} %copy-done.7, ...), kind=kOutput, calls=%fused_computation.35 | convolution fusion | flops 841644544 | bytes 8204288 | tf_op jit(solution)/shard_map/tc,rc->tr/dot_general | solution.py:32
  99.2 0.3 fusion.23
  99.6 29.2 %all-gather.8.cloned.1.call-done = bf16[1280,1280]{1,0:T(8,128)(2,1)} async-done(((bf16[160,1280]{1,0:T(8,128)(2,1)}), bf16[1280,1280]{1,0:T(8,128)(2,1)}) %all-gather.8.cloned.1.call-update) | async-done | bytes 3276816 | tf_op jit(solution)/shard_map/all_gather | solution.py:164
  128.8 3.1 %convolution_convert_fusion = bf16[128,1280]{1,0:T(8,128)(2,1)S(1)} fusion(bf16[128,1280]{1,0:T(8,128)(2,1)S(1)} %fusion.23, bf16[1280,1280]{1,0:T(8,128)(2,1)} %all-gather.8.cloned.1.call-done), kind=kOutput, calls=%fused_computation.9 | convolution fusion | flops 419594240 | bytes 3932160 | tf_op jit(solution)/shard_map/tc,rc->tr/dot_general | solution.py:32
  132.0 0.9 copy.27
  132.9 4.6 %all-to-all-start = ((bf16[128,4,320]{0,2,1:T(8,128)(2,1)}), bf16[128,4,320]{0,2,1:T(8,128)(2,1)S(1)}, u32[]{:S(2)}, u32[]{:S(2)}) async-start(bf16[128,4,320]{0,2,1:T(8,128)(2,1)} %bitcast.4), calls=%async_computation | async-start | bytes 655360 | tf_op jit(solution)/shard_map/all_to_all | solution.py:166
  137.5 0.8 multiply_reduce_fusion.19
  138.6 0.8 multiply_reduce_fusion.13
  139.5 2.7 stack.127
  142.2 40.2 %psum.15 = f32[1280]{0:T(1024)} all-reduce(f32[1280]{0:T(1024)S(1)} %get-tuple-element.66), channel_id=1, replica_groups=mesh['dp'=8,'seq'=4] {'dp','seq'}, use_global_device_ids=true, to_apply=%region_43.44 | all-reduce | flops 1280 | bytes 10240 | tf_op jit(solution)/shard_map/psum | solution.py:169
  182.4 0.3 copy.28
  182.7 0.1 reshape.152
  182.8 3.8 %fusion.11 = bf16[4,80,512]{2,1,0:T(8,128)(2,1)} fusion(bf16[512,4,80]{0,2,1:T(8,128)(2,1)S(1)} %reshape.152, f32[4,512,512]{1,2,0:T(8,128)} %get-tuple-element.139, f32[4,512]{1,0:T(4,128)S(1)} %get-tuple-element.138), kind=kOutput, calls=%fused_computation.20 | convolution fusion | flops 170033152 | bytes 4857856 | tf_op jit(solution)/shard_map/while/body/eval_jaxpr/hqk,qhd->khd/dot_general | solution.py:61
  186.7 0.8 multiply_reduce_fusion
  187.4 1.2 multiply_convert_fusion
  188.6 1.5 fusion.9
  190.1 1.2 fusion.10
  191.3 75.2 %all-reduce.2.cloned.1.call-done = f32[31,1280]{1,0:T(8,128)} async-done(((f32[31,1280]{1,0:T(8,128)}), f32[31,1280]{1,0:T(8,128)}) %all-reduce.2.cloned.1.call-update) | async-done | bytes 158736 | tf_op jit(solution)/shard_map/psum | solution.py:169
  266.5 1.6 copy.36
  (68 shorter events, 0.7 us)
Async XLA Ops:
  7.2 14.7 %copy-start = (bf16[512,320]{0,1:T(8,128)(2,1)S(1)}, bf16[512,320]{0,1:T(8,128)(2,1)}, u32[]{:S(2)}) copy-start(bf16[512,320]{0,1:T(8,128)(2,1)} %param.15) | copy-start | bytes 983044
  7.2 38.3 %all-gather.4.cloned.1.call-start = ((), (), s32[]{:S(2)}) async-start(), calls=%async_computation.1 | async-start | bytes 3686400 | tf_op jit(solution)/shard_map/all_gather | solution.py:131
  7.9 86.1 %all-gather.6.cloned.1.call-start = ((), (), s32[]{:S(2)}) async-start(), calls=%async_computation.2 | async-start | bytes 7372800 | tf_op jit(solution)/shard_map/all_gather | solution.py:151
  8.7 120.2 %all-gather.8.cloned.1.call-start = ((), (), s32[]{:S(2)}) async-start(), calls=%async_computation.3 | async-start | bytes 3686400 | tf_op jit(solution)/shard_map/all_gather | solution.py:164
  10.0 18.0 %collective-permute-start = (bf16[15,1280]{1,0:T(8,128)(2,1)S(1)}, bf16[15,1280]{1,0:T(8,128)(2,1)S(1)}, u32[]{:S(2)}, u32[]{:S(2)}) collective-permute-start(bf16[15,1280]{1,0:T(8,128)(2,1)S(1)} %get-tuple-element.105), channel_id=1, source_target_pairs={{0,1},{1,2},{2,3},{4,5},{5,6},{6,7},{8,9},{9,10},{10,11},{12,13},{... | collective-permute-start | bytes 115208 | tf_op jit(solution)/shard_map/ppermute | solution.py:17
  14.9 13.1 %collective-permute-start.1 = (bf16[15,1280]{1,0:T(8,128)(2,1)S(1)}, bf16[15,1280]{1,0:T(8,128)(2,1)S(1)}, u32[]{:S(2)}, u32[]{:S(2)}) collective-permute-start(bf16[15,1280]{1,0:T(8,128)(2,1)S(1)} %get-tuple-element.106), channel_id=1, source_target_pairs={{1,0},{2,1},{3,2},{5,4},{6,5},{7,6},{9,8},{10,9},{11,10},{13,12},{... | collective-permute-start | bytes 115208 | tf_op jit(solution)/shard_map/ppermute | solution.py:20
  21.8 23.7 %copy-start.5 = (bf16[128,1280]{1,0:T(8,128)(2,1)S(1)}, bf16[128,1280]{1,0:T(8,128)(2,1)}, u32[]{:S(2)}) copy-start(bf16[128,1280]{1,0:T(8,128)(2,1)} %param.12) | copy-start | bytes 983044
  51.1 5.1 %collective-permute-start.2 = (bf16[15,1280]{1,0:T(8,128)(2,1)S(1)}, bf16[15,1280]{1,0:T(8,128)(2,1)S(1)}, u32[]{:S(2)}, u32[]{:S(2)}) collective-permute-start(bf16[15,1280]{1,0:T(8,128)(2,1)S(1)} %get-tuple-element.103), channel_id=1, source_target_pairs={{0,1},{1,2},{2,3},{4,5},{5,6},{6,7},{8,9},{9,10},{10,11},{12,13},{... | collective-permute-start | bytes 115208 | tf_op jit(solution)/shard_map/ppermute | solution.py:17
  54.5 5.9 %collective-permute-start.3 = (bf16[15,1280]{1,0:T(8,128)(2,1)S(1)}, bf16[15,1280]{1,0:T(8,128)(2,1)S(1)}, u32[]{:S(2)}, u32[]{:S(2)}) collective-permute-start(bf16[15,1280]{1,0:T(8,128)(2,1)S(1)} %get-tuple-element.104), channel_id=1, source_target_pairs={{1,0},{2,1},{3,2},{5,4},{6,5},{7,6},{9,8},{10,9},{11,10},{13,12},{... | collective-permute-start | bytes 115208 | tf_op jit(solution)/shard_map/ppermute | solution.py:20
  61.3 1.8 copy-start.2
  63.1 30.9 %copy-start.3 = (bf16[128,1280]{1,0:T(8,128)(2,1)S(1)}, bf16[128,1280]{1,0:T(8,128)(2,1)}, u32[]{:S(2)}) copy-start(bf16[128,1280]{1,0:T(8,128)(2,1)} %param.13) | copy-start | bytes 983044
  63.1 30.9 %copy-start.7 = (f32[1280]{0:T(1024)S(1)}, f32[1280]{0:T(1024)}, u32[]{:S(2)}) copy-start(f32[1280]{0:T(1024)} %param.19) | copy-start | bytes 15364
  99.6 38.7 %copy-start.4 = (bf16[128,1280]{1,0:T(8,128)(2,1)}, bf16[128,1280]{1,0:T(8,128)(2,1)S(1)}, u32[]{:S(2)}) copy-start(bf16[128,1280]{1,0:T(8,128)(2,1)S(1)} %fusion.23) | copy-start | bytes 983044
  132.9 49.5 %all-to-all-start = ((bf16[128,4,320]{0,2,1:T(8,128)(2,1)}), bf16[128,4,320]{0,2,1:T(8,128)(2,1)S(1)}, u32[]{:S(2)}, u32[]{:S(2)}) async-start(bf16[128,4,320]{0,2,1:T(8,128)(2,1)} %bitcast.4), calls=%async_computation | async-start | bytes 655360 | tf_op jit(solution)/shard_map/all_to_all | solution.py:166
  137.5 129.1 %all-reduce.2.cloned.1.call-start = ((), (), s32[]{:S(2)}) async-start(), calls=%async_computation.4 | async-start | bytes 327680 | tf_op jit(solution)/shard_map/psum | solution.py:169
  182.8 3.9 %copy-start.1 = (f32[4,512,512]{1,2,0:T(8,128)S(1)}, f32[4,512,512]{1,2,0:T(8,128)}, u32[]{:S(2)}) copy-start(f32[4,512,512]{1,2,0:T(8,128)} %get-tuple-element.139) | copy-start | bytes 12582916
  182.8 3.9 %copy-start.8 = (bf16[512,320]{0,1:T(8,128)(2,1)S(1)}, bf16[512,320]{0,1:T(8,128)(2,1)}, u32[]{:S(2)}) copy-start(bf16[512,320]{0,1:T(8,128)(2,1)} %param.17) | copy-start | bytes 983044
  187.4 2.7 copy-start.6
Sparse Core Ops, SparseCore 0:
  9.9 35.5 all-gather.3
  47.4 46.6 all-gather.5
  95.9 32.8 all-gather.7
  144.1 122.3 all-reduce.1
where the time goes:
time: 277 us; the launch traced here: 275 us
  waiting for transfers between devices  154 us (56%)
  blocking collectives  40.2 us (15%)
  matrix products  25.9 us (9%)
  starting transfers between devices  15.8 us (6%)
  other arithmetic  15.2 us (5%)
  between operations  14.3 us (5%)
  local copies, waits for them, and re-layouts  8.78 us (3%)
    psum x1, waiting for transfers between devices, local(): lax.psum((jnp.stack(kernel_rows), gain_term), ('dp', 'seq'))  75.2 us
    psum x1, blocking collectives, local(): lax.psum((jnp.stack(kernel_rows), gain_term), ('dp', 'seq'))  40.2 us
    all_gather x1, waiting for transfers between devices, local(): lax.all_gather(w_attn_out, 'dp', axis=0, tiled=True)  29.2 us
    all_gather x1, waiting for transfers between devices, local(): lax.all_gather(w_in, 'dp', axis=0, tiled=True)  26.8 us
    all_gather x1, waiting for transfers between devices, local(): lax.all_gather(w_conv_out, 'dp', axis=0, tiled=True)  17.4 us
    dot_general x3, matrix products, row_product(): jnp.einsum('tc,rc->tr', active, piece, preferred_element_type=jnp.float32)  13.9 us
    ppermute x2, starting transfers between devices, padded(): lax.ppermute(lax.slice_in_dim(block, block.shape[dim] - width, None, axis...  8.32 us
  transfers between devices with their start and end apart: 9, of which 6 were waited for; matrix products, arithmetic and copies ran while one was open for 16% of the time, Pallas kernels for 0%

commit v1 on v0

--- a/solution.py
+++ b/solution.py
@@ -3,6 +3,8 @@
 import jax
 import jax.numpy as jnp
 from jax import lax
+from jax.experimental import pallas as pl
+from jax.experimental.pallas import tpu as pltpu
 from jax.sharding import PartitionSpec as P
 
 HD = 80
@@ -170,6 +172,409 @@
     return (resid_grad, query_grad, key_grad, value_grad, kernel_grad, gain_grad)
 
 
+MESH = pl.DeviceIdType.MESH
+NT = (((1,), (1,)), ((), ()))
+NN = (((1,), (0,)), ((), ()))
+TN = (((0,), (0,)), ((), ()))
+PART = 48
+LANES = 128
+COPIES = 59
+
+
+def fused(
+    go_ref, x_ref, pre_ref, q_ref, k_ref, v_ref, counts_ref, gain_ref, kern_ref,
+    w_in_ref, w_conv_ref, w_attn_ref,
+    resid_ref, qg_ref, kg_ref, vg_ref, taps_ref, gaing_ref,
+    full_conv, full_in, full_attn, glu_ref, gext_ref, halo_ref, seg_ref, segc_ref,
+    conv_ref, cog_ref, cg_ref, cext_ref, gin_ref, ng_ref, probs_ref, ctx_ref, dout_ref,
+    qa_ref, ka_ref, va_ref, sums_ref, part_a, mine_a, part_b, total_ref,
+    send_sem, recv_sem, local_sem,
+):
+    f32, bf16 = jnp.float32, jnp.bfloat16
+    rows, width = go_ref.shape
+    total, cols = q_ref.shape
+    heads = cols // HD
+    n_seq = total // rows
+    n_dp = 8
+    shard = width // n_dp
+    half = KW // 2
+    me, z = lax.axis_index("dp"), lax.axis_index("seq")
+    core = me % 2
+    sib = me + 1 - 2 * core
+    xn = me + 2 - 4 * ((me // 2) % 2)
+    yn = me + 4 - 8 * (me // 4)
+    diag = xn + 4 - 8 * (me // 4)
+    over = 1 - 2 * core
+    zn = z + 1 - 2 * (z % 2)
+    moff = PART * (z % 2)
+    toff = PART - moff
+
+    barrier = pltpu.get_barrier_semaphore()
+    for s in range(1, n_dp):
+        pl.semaphore_signal(barrier, inc=1, device_id=((me + s) % n_dp, z), device_id_type=MESH)
+    for s in range(1, n_seq):
+        pl.semaphore_signal(barrier, inc=1, device_id=(me, (z + s) % n_seq), device_id_type=MESH)
+    pl.semaphore_wait(barrier, n_dp + n_seq - 2)
+
+    sent = []
+
+    def remote(src, dst, idx, dp, seq):
+        return pltpu.make_async_remote_copy(
+            src_ref=src, dst_ref=dst, send_sem=send_sem.at[idx], recv_sem=recv_sem.at[idx],
+            device_id=(dp, seq), device_id_type=MESH,
+        )
+
+    def push(src, dst, idx, dp, seq):
+        copy = remote(src, dst, idx, dp, seq)
+        copy.start()
+        sent.append(copy)
+
+    def arrive(dst, idx):
+        remote(dst, dst, idx, sib, z).wait_recv()
+
+    weights = ((w_conv_ref, full_conv), (w_in_ref, full_in), (w_attn_ref, full_attn))
+
+    def span(start, size):
+        return pl.ds(pl.multiple_of(start, 16), size)
+
+    def piece(m, owner, off, size):
+        return weights[m][1].at[span(owner * shard + off, size), :]
+
+    rest = shard - 2 * PART
+    own_copies = [
+        pltpu.make_async_copy(weights[m][0], piece(m, me, 0, shard), local_sem.at[m])
+        for m in range(3)
+    ]
+
+    def send_own(m):
+        base = 13 * m
+        source = weights[m][0]
+        for k, dev in ((0, xn), (2, yn)):
+            push(source.at[span(moff, PART), :], piece(m, me, moff, PART), base + k, dev, z)
+            push(source.at[pl.ds(2 * PART, rest), :], piece(m, me, 2 * PART, rest), base + k + 1, dev, z)
+        push(source, piece(m, me, 0, shard), base + 9, sib, z)
+        own_copies[m].start()
+
+    def forward_xy(m):
+        base = 13 * m
+        for k, dev in ((0, xn), (2, yn)):
+            arrive(piece(m, dev, moff, PART), base + k)
+            arrive(piece(m, dev, 2 * PART, rest), base + k + 1)
+        via = core * yn + (1 - core) * xn
+        owner = core * xn + (1 - core) * yn
+        for k, off, size in ((4, moff, PART), (5, 2 * PART, rest)):
+            push(piece(m, owner, off, size), piece(m, owner, off, size), base + k, via, z)
+        for k, dev in ((6, xn), (7, yn)):
+            push(piece(m, dev, moff, PART), piece(m, dev, moff, PART), base + k, me, zn)
+
+    def forward_diag(m):
+        base = 13 * m
+        arrive(piece(m, diag, moff, PART), base + 4)
+        push(piece(m, diag, moff, PART), piece(m, diag, moff, PART), base + 8, me, zn)
+        arrive(piece(m, diag, 2 * PART, rest), base + 5)
+        for k, dev in ((6, xn), (7, yn)):
+            arrive(piece(m, dev, toff, PART), base + k)
+            push(piece(m, dev, 0, shard), piece(m, dev, 0, shard), base + k + 4, sib, z)
+
+    def finish(m):
+        base = 13 * m
+        arrive(piece(m, diag, toff, PART), base + 8)
+        push(piece(m, diag, 0, shard), piece(m, diag, 0, shard), base + 12, sib, z)
+        for k, dev in ((9, sib), (10, xn + over), (11, yn + over), (12, diag + over)):
+            arrive(piece(m, dev, 0, shard), base + k)
+        own_copies[m].wait()
+
+    def segments(pos):
+        end = jnp.int32(0)
+        seg = jnp.zeros(pos.shape, jnp.int32)
+        for u in range(counts_ref.shape[1]):
+            end = end + counts_ref[0, u]
+            seg = seg + jnp.where(pos >= end, 1, 0)
+        return jnp.where(pos < 0, -1, seg)
+
+    def tiles(n, size):
+        return pl.ds(pl.multiple_of(n * size, size), size)
+
+    prev, following = (z + n_seq - 1) % n_seq, (z + 1) % n_seq
+
+    def send_halo(src, slot, idx):
+        push(src.at[pl.ds(rows - 16, 16), :], halo_ref.at[slot], idx, me, following)
+        push(src.at[pl.ds(0, 16), :], halo_ref.at[slot + 1], idx + 1, me, prev)
+
+    def take_halo(dst, slot, idx):
+        arrive(halo_ref.at[slot], idx)
+        arrive(halo_ref.at[slot + 1], idx + 1)
+        dst[0:16, :] = halo_ref[slot].astype(f32)
+        dst[rows + 16 : rows + 32, :] = halo_ref[slot + 1].astype(f32)
+
+    send_own(0)
+
+    @pl.loop(0, width // LANES)
+    def _(n):
+        c = tiles(n, LANES)
+        c2 = pl.ds(pl.multiple_of(width + n * LANES, LANES), LANES)
+        gate = jax.nn.sigmoid(pre_ref[:, c2].astype(f32))
+        glu = (pre_ref[:, c].astype(f32) * gate).astype(bf16)
+        glu_ref[:, c] = glu
+        gext_ref[16 : 16 + rows, c] = glu.astype(f32)
+
+    send_halo(glu_ref, 0, 39)
+
+    seg_ref[...] = segments(
+        z * rows - 16 + lax.broadcasted_iota(jnp.int32, (rows + 32, LANES), 0)
+    )
+    segc_ref[...] = segments(lax.broadcasted_iota(jnp.int32, (total, LANES), 0))
+
+    scale = 1.0 / math.sqrt(HD)
+    qblock = 256
+
+    def window(h):
+        low = h * HD // LANES * LANES
+        high = min(-(-(h + 1) * HD // LANES) * LANES, cols)
+        lane = low + lax.broadcasted_iota(jnp.int32, (1, high - low), 1)
+        inside = jnp.where((lane >= h * HD) & (lane < (h + 1) * HD), 1.0, 0.0).astype(bf16)
+        return low, high, inside
+
+    def make_probs(h):
+        low, high, inside = window(h)
+
+        @pl.loop(0, total // qblock)
+        def _(b):
+            queries = q_ref[tiles(b, qblock), low:high]
+            scores = (
+                lax.dot_general(k_ref[:, low:high] * inside, queries, NT, preferred_element_type=f32)
+                * scale
+            )
+            seg_q = segments(b * qblock + lax.broadcasted_iota(jnp.int32, (1, qblock), 1))
+            seg_k = jnp.concatenate([segc_ref[...]] * (qblock // LANES), axis=1)
+            scores = jnp.where(seg_k == seg_q, scores, -1e30)
+            expd = jnp.exp(scores - jnp.max(scores, axis=0, keepdims=True))
+            probs_ref[h, b] = expd * (1.0 / jnp.sum(expd, axis=0, keepdims=True))
+
+    make_probs(0)
+    forward_xy(0)
+    send_own(1)
+
+    take_halo(gext_ref, 0, 39)
+
+    @pl.loop(0, width // LANES)
+    def _(n):
+        c = tiles(n, LANES)
+        seg_own = seg_ref[16 : 16 + rows, :]
+        acc = jnp.zeros((rows, LANES), f32)
+        for o in range(KW):
+            same = seg_ref[o + 1 : o + 1 + rows, :] == seg_own
+            acc = acc + kern_ref[o : o + 1, c] * jnp.where(
+                same, gext_ref[o + 1 : o + 1 + rows, c], 0.0
+            )
+        conv_ref[:, c] = acc
+
+    forward_diag(0)
+    for h in range(1, heads):
+        make_probs(h)
+    finish(0)
+
+    @pl.loop(0, width // 256)
+    def _(n):
+        c = tiles(n, 256)
+        cog_ref[:, c] = lax.dot_general(go_ref[...], full_conv[c, :], NT, preferred_element_type=f32)
+
+    @pl.loop(0, width // LANES)
+    def _(n):
+        c = tiles(n, LANES)
+        conv = conv_ref[:, c]
+        sig = jax.nn.sigmoid(conv)
+        grad = (cog_ref[:, c] * sig * (1.0 + conv * (1.0 - sig))).astype(bf16)
+        cg_ref[:, c] = grad
+        cext_ref[16 : 16 + rows, c] = grad.astype(f32)
+
+    send_halo(cg_ref, 2, 41)
+    forward_xy(1)
+    send_own(2)
+    take_halo(cext_ref, 2, 41)
+
+    @pl.loop(0, width // LANES)
+    def _(n):
+        c = tiles(n, LANES)
+        c2 = pl.ds(pl.multiple_of(width + n * LANES, LANES), LANES)
+        seg_own = seg_ref[16 : 16 + rows, :]
+        grad_own = cext_ref[16 : 16 + rows, c]
+        acc = jnp.zeros((rows, LANES), f32)
+        for o in range(KW):
+            same = seg_ref[o + 1 : o + 1 + rows, :] == seg_own
+            near = jnp.where(same, cext_ref[o + 1 : o + 1 + rows, c], 0.0)
+            acc = acc + kern_ref[KW - 1 - o : KW - o, c] * near
+            pair = jnp.where(same, grad_own * gext_ref[o + 1 : o + 1 + rows, c], 0.0)
+            sums_ref[o : o + 1, c] = jnp.sum(pair, axis=0, keepdims=True)
+        gate = jax.nn.sigmoid(pre_ref[:, c2].astype(f32))
+        scaled = acc * gate
+        gin_ref[:, c] = scaled.astype(bf16)
+        gin_ref[:, c2] = (scaled * pre_ref[:, c].astype(f32) * (1.0 - gate)).astype(bf16)
+
+    forward_diag(1)
+    finish(1)
+
+    @pl.loop(0, width // 256)
+    def _(n):
+        c = tiles(n, 256)
+        ng_ref[:, c] = lax.dot_general(gin_ref[...], full_in[c, :], NT, preferred_element_type=f32)
+
+    forward_xy(2)
+    sums_ref[KW : KW + 1, :] = jnp.zeros((1, width), f32)
+
+    @pl.loop(0, rows // 16)
+    def _(n):
+        r = tiles(n, 16)
+        x = x_ref[r, :].astype(f32)
+        centred = x - jnp.mean(x, axis=1, keepdims=True)
+        inv = 1.0 / jnp.sqrt(jnp.mean(centred * centred, axis=1, keepdims=True) + 1e-05)
+        normed = centred * inv
+        grad = ng_ref[r, :]
+        scaled = grad * gain_ref[...]
+        back = inv * (
+            scaled
+            - jnp.mean(scaled, axis=1, keepdims=True)
+            - normed * jnp.mean(scaled * normed, axis=1, keepdims=True)
+        )
+        resid_ref[r, :] = (go_ref[r, :].astype(f32) + back).astype(bf16)
+        sums_ref[KW : KW + 1, :] += jnp.sum(grad * normed, axis=0, keepdims=True)
+
+    forward_diag(2)
+    for s in range(1, n_seq):
+        to = (z + s) % n_seq
+        push(sums_ref.at[tiles(to, 8), :], part_a.at[s - 1], 45 + s, me, to)
+    finish(2)
+
+    for s in range(1, n_seq + 1):
+        to = (z + s) % n_seq
+        out = lax.dot_general(
+            resid_ref[...], full_attn[tiles(to, cols), :], NT, preferred_element_type=f32
+        ).astype(bf16)
+        if s < n_seq:
+            ctx_ref[s - 1] = out
+            push(ctx_ref.at[s - 1], dout_ref.at[tiles(z, rows), :], 42 + s, me, to)
+        else:
+            dout_ref[tiles(z, rows), :] = out
+
+    for s in range(1, n_seq):
+        arrive(part_a.at[s - 1], 45 + s)
+    mine_a[...] = sums_ref[tiles(z, 8), :] + part_a[0] + part_a[1] + part_a[2]
+    for s in range(1, n_dp):
+        push(mine_a, part_b.at[me], 48 + s, (me + s) % n_dp, z)
+    part_b[me] = mine_a[...]
+
+    for s in range(1, n_seq):
+        arrive(dout_ref.at[tiles((z + n_seq - s) % n_seq, rows), :], 42 + s)
+
+    qa_ref[...] = jnp.zeros((total, cols), f32)
+    ka_ref[...] = jnp.zeros((total, cols), f32)
+    va_ref[...] = jnp.zeros((total, cols), f32)
+    for h in range(heads):
+        low, high, inside = window(h)
+
+        @pl.loop(0, total // qblock)
+        def _(b):
+            r = tiles(b, qblock)
+            probs = probs_ref[h, b]
+            dout = dout_ref[r, low:high] * inside
+            va_ref[:, low:high] += lax.dot_general(
+                probs.astype(bf16), dout, NN, preferred_element_type=f32
+            )
+            prob_grad = lax.dot_general(v_ref[:, low:high], dout, NT, preferred_element_type=f32)
+            delta = jnp.sum(probs * prob_grad, axis=0, keepdims=True)
+            score_grad = (probs * (prob_grad - delta)).astype(bf16)
+            ka_ref[:, low:high] += lax.dot_general(
+                score_grad, q_ref[r, low:high] * inside, NN, preferred_element_type=f32
+            )
+            qa_ref[r, low:high] += lax.dot_general(
+                score_grad, k_ref[:, low:high] * inside, TN, preferred_element_type=f32
+            )
+
+        if h == 1:
+            for s in range(1, n_dp):
+                arrive(part_b.at[(me + n_dp - s) % n_dp], 48 + s)
+            chunk = part_b[0]
+            for i in range(1, n_dp):
+                chunk = chunk + part_b[i]
+            total_ref[tiles(z, 8), :] = chunk
+            for s in range(1, n_seq):
+                block = total_ref.at[tiles(z, 8), :]
+                push(block, block, 55 + s, me, (z + s) % n_seq)
+
+    qg_ref[...] = (qa_ref[...] * scale).astype(bf16)
+    kg_ref[...] = (ka_ref[...] * scale).astype(bf16)
+    vg_ref[...] = va_ref[...].astype(bf16)
+    for s in range(1, n_seq):
+        arrive(total_ref.at[tiles((z + n_seq - s) % n_seq, 8), :], 55 + s)
+    taps_ref[...] = total_ref[0:KW, :]
+    gaing_ref[...] = total_ref[KW : KW + 1, :]
+    for copy in sent:
+        copy.wait_send()
+
+
+def fused_local(
+    grad_out, saved_input, pre_glu, queries, keys, values, frame_counts, norm_gain, kernel,
+    w_in, w_conv_out, w_attn_out,
+):
+    rows, width = grad_out.shape
+    total, cols = queries.shape
+    heads = cols // HD
+    f32, bf16 = jnp.float32, jnp.bfloat16
+    vmem = pl.BlockSpec(memory_space=pltpu.VMEM)
+    smem = pl.BlockSpec(memory_space=pltpu.SMEM)
+    hbm = pl.BlockSpec(memory_space=pl.ANY)
+    outs = pl.pallas_call(
+        fused,
+        out_shape=(
+            jax.ShapeDtypeStruct((rows, width), bf16),
+            jax.ShapeDtypeStruct((total, cols), bf16),
+            jax.ShapeDtypeStruct((total, cols), bf16),
+            jax.ShapeDtypeStruct((total, cols), bf16),
+            jax.ShapeDtypeStruct((KW, width), f32),
+            jax.ShapeDtypeStruct((1, width), f32),
+        ),
+        in_specs=[vmem] * 6 + [smem] + [vmem] * 2 + [hbm] * 3,
+        out_specs=(vmem,) * 6,
+        scratch_shapes=[
+            pltpu.VMEM((width, width), bf16),
+            pltpu.VMEM((width, 2 * width), bf16),
+            pltpu.VMEM((width, width), bf16),
+            pltpu.VMEM((rows, width), bf16),
+            pltpu.VMEM((rows + 32, width), f32),
+            pltpu.VMEM((4, 16, width), bf16),
+            pltpu.VMEM((rows + 32, LANES), jnp.int32),
+            pltpu.VMEM((total, LANES), jnp.int32),
+            pltpu.VMEM((rows, width), f32),
+            pltpu.VMEM((rows, width), f32),
+            pltpu.VMEM((rows, width), bf16),
+            pltpu.VMEM((rows + 32, width), f32),
+            pltpu.VMEM((rows, 2 * width), bf16),
+            pltpu.VMEM((rows, width), f32),
+            pltpu.VMEM((heads, total // 256, total, 256), f32),
+            pltpu.VMEM((3, rows, cols), bf16),
+            pltpu.VMEM((total, cols), bf16),
+            pltpu.VMEM((total, cols), f32),
+            pltpu.VMEM((total, cols), f32),
+            pltpu.VMEM((total, cols), f32),
+            pltpu.VMEM((KW + 1, width), f32),
+            pltpu.VMEM((3, 8, width), f32),
+            pltpu.VMEM((8, width), f32),
+            pltpu.VMEM((8, 8, width), f32),
+            pltpu.VMEM((KW + 1, width), f32),
+            pltpu.SemaphoreType.DMA((COPIES,)),
+            pltpu.SemaphoreType.DMA((COPIES,)),
+            pltpu.SemaphoreType.DMA((3,)),
+        ],
+        compiler_params=pltpu.CompilerParams(
+            collective_id=0, has_side_effects=True, vmem_limit_bytes=50 * 1024 * 1024
+        ),
+    )(
+        grad_out, saved_input, pre_glu, queries, keys, values, frame_counts,
+        norm_gain.reshape(1, width), kernel, w_in, w_conv_out, w_attn_out,
+    )
+    return outs[:5] + (outs[5].reshape(width),)
+
+
 def solution(mesh):
     in_specs = (
         P(("dp", "seq"), None),
@@ -186,4 +591,6 @@
         P("dp", None),
     )
     out_specs = (P(("dp", "seq"), None), P("dp", "seq"), P("dp", "seq"), P("dp", "seq"), P(), P())
-    return jax.shard_map(local, mesh=mesh, in_specs=in_specs, out_specs=out_specs, check_vma=False)
+    small = mesh.shape["dp"] == 8 and mesh.shape["seq"] == 4
+    body = fused_local if small else local
+    return jax.shard_map(body, mesh=mesh, in_specs=in_specs, out_specs=out_specs, check_vma=False)

time: 277 us -> 97.5 us (0.35)
  waiting for transfers between devices: 154 us -> 0 us
  Pallas kernels: 0 us -> 85.9 us
  blocking collectives: 40.2 us -> 0 us
  matrix products: 25.9 us -> 0 us
  starting transfers between devices: 15.8 us -> 0 us
  other arithmetic: 15.2 us -> 0.62 us
  between operations: 14.3 us -> 0.73 us
    pallas_call x0 -> x1, Pallas kernels: none -> 85.9 us  [fused_local(): pl.pallas_call(fused, out_shape=(jax.ShapeDtypeStruct((rows, width), bf16...]
    psum x1 -> x0, waiting for transfers between devices: 75.2 us -> none  [local(): lax.psum((jnp.stack(kernel_rows), gain_term), ('dp', 'seq'))]
    all_gather x3 -> x0, waiting for transfers between devices: 73.4 us -> none  [the longest x1 29.2 us: local(): lax.all_gather(w_attn_out, 'dp', axis=0, tiled=True)]
    psum x1 -> x0, blocking collectives: 40.2 us -> none  [local(): lax.psum((jnp.stack(kernel_rows), gain_term), ('dp', 'seq'))]
    dot_general x7 -> x0, matrix products: 21.1 us -> none  [the longest x3 13.9 us: row_product(): jnp.einsum('tc,rc->tr', active, piece, preferred_element_type=jnp.float32)]
    ppermute x4 -> x0, starting transfers between devices: 11.1 us -> none  [the longest x2 8.32 us: padded(): lax.ppermute(lax.slice_in_dim(block, block.shape[dim] - width, None, axis...]
    unnamed x19 -> x30, local copies, waits for them, and re-layouts: 1.65 us -> 9.27 us
    reduce_sum x9 -> x0, other arithmetic: 6.73 us -> none  [the longest x5 4.18 us: local(): jnp.sum(grad_float * glu_ext[tap_index:tap_index + t_dev] * matches[tap_i...]
  transfers between devices with their start and end apart: 9 -> 0, of which waited for: 6 -> 0; matrix products, arithmetic and copies ran while one was open for 16% -> 0% of each run, Pallas kernels for 0% -> 0%
where the time goes in v1:
time: 97.5 us; the launch traced here: 97.2 us
  Pallas kernels  85.9 us (88%)
  local copies, waits for them, and re-layouts  9.97 us (10%)
    pallas_call x1, Pallas kernels, fused_local(): pl.pallas_call(fused, out_shape=(jax.ShapeDtypeStruct((rows, width), bf16...  85.9 us
    unnamed x30, local copies, waits for them, and re-layouts  9.27 us

profile of v1, /device:TPU:0, one launch (start us, length us, event | category | flops | bytes accessed | tf_op | source)
XLA Modules:
  0.0 97.2 jit_solution(15936404823813912875)
XLA Ops:
  0.6 0.7 reshape.18.gain_ref
  1.3 0.0 copy-start.9
  1.3 0.0 copy-start.10
  1.3 1.2 %copy.18.q_ref = bf16[512,320]{1,0:T(8,128)(2,1)S(1)} copy(bf16[512,320]{0,1:T(8,128)(2,1)} %param.15) | data formatting | bytes 655360 | tf_op args[3]
  2.6 0.0 copy-done.9
  2.6 0.0 copy-start.1
  2.6 0.0 copy-start.2
  2.6 0.2 copy.19.k_ref
  2.8 0.0 copy-done.10
  2.9 0.0 copy-start
  2.9 0.0 copy-start.8
  2.9 0.2 copy.20.v_ref
  3.1 0.5 copy-done.1
  3.6 0.1 copy-done.2
  3.7 0.2 copy-done
  3.9 0.0 copy-done.8
  3.9 0.0 copy-start.5
  3.9 0.9 copy-done.5
  4.8 85.9 %shard_map.163 = (bf16[128,1280]{1,0:T(8,128)(2,1)S(1)}, bf16[512,320]{1,0:T(8,128)(2,1)S(1)}, bf16[512,320]{1,0:T(8,128)(2,1)S(1)}, bf16[512,320]{1,0:T(8,128)(...) custom-call(bf16[128,1280]{1,0:T(8,128)(2,1)S(1)} %copy-done.1, bf16[128,1280]{1,0:T(8,128)(2,1)S(1)} %copy-done.2, ...), custom_call_target="tpu_custom_call" | custom-call | tf_op jit(solution)/shard_map/pallas_call | solution.py:526
  90.7 0.0 copy-start.3
  90.7 0.7 copy-done.3
  91.4 0.0 copy-start.6
  91.4 0.7 copy-done.6
  92.1 0.6 reduce
  92.7 0.9 copy.21
  93.6 0.9 copy.22
  94.5 0.0 copy-start.4
  94.5 0.9 copy.23
  95.4 0.1 copy-done.4
  95.5 0.0 copy-start.7
  95.5 0.7 copy.26
  96.2 0.3 copy-done.7
  96.5 0.7 copy.27
Async XLA Ops:
  1.3 1.3 %copy-start.9 = (bf16[512,320]{0,1:T(8,128)(2,1)S(1)}, bf16[512,320]{0,1:T(8,128)(2,1)}, u32[]{:S(2)}) copy-start(bf16[512,320]{0,1:T(8,128)(2,1)} %param.16) | copy-start | bytes 983044
  1.3 1.5 %copy-start.10 = (bf16[512,320]{0,1:T(8,128)(2,1)S(1)}, bf16[512,320]{0,1:T(8,128)(2,1)}, u32[]{:S(2)}) copy-start(bf16[512,320]{0,1:T(8,128)(2,1)} %param.17) | copy-start | bytes 983044
  2.6 1.0 %copy-start.1 = (bf16[128,1280]{1,0:T(8,128)(2,1)S(1)}, bf16[128,1280]{1,0:T(8,128)(2,1)}, u32[]{:S(2)}) copy-start(bf16[128,1280]{1,0:T(8,128)(2,1)} %go_ref.1) | copy-start | bytes 983044
  2.6 1.1 %copy-start.2 = (bf16[128,1280]{1,0:T(8,128)(2,1)S(1)}, bf16[128,1280]{1,0:T(8,128)(2,1)}, u32[]{:S(2)}) copy-start(bf16[128,1280]{1,0:T(8,128)(2,1)} %x_ref.1) | copy-start | bytes 983044
  2.9 1.1 %copy-start = (bf16[160,1280]{1,0:T(8,128)(2,1)S(1)}, bf16[160,1280]{1,0:T(8,128)(2,1)}, u32[]{:S(2)}) copy-start(bf16[160,1280]{1,0:T(8,128)(2,1)} %w_conv_ref.1) | copy-start | bytes 1228804
  2.9 1.0 %copy-start.8 = (s32[1,8]{1,0:T(1,128)S(1)}, s32[1,8]{1,0:T(1,128)}, u32[]{:S(2)}) copy-start(s32[1,8]{1,0:T(1,128)} %counts_ref.1) | copy-start | bytes 100
  3.9 0.9 copy-start.5
  90.7 0.7 copy-start.3
  91.4 0.7 copy-start.6
  94.5 1.0 %copy-start.4 = (bf16[128,1280]{1,0:T(8,128)(2,1)S(1)}, bf16[128,1280]{1,0:T(8,128)(2,1)}, u32[]{:S(2)}) copy-start(bf16[128,1280]{1,0:T(8,128)(2,1)} %copy-done.3) | copy-start | bytes 983044
  95.5 1.0 %copy-start.7 = (f32[31,1280]{1,0:T(8,128)S(1)}, f32[31,1280]{1,0:T(8,128)}, u32[]{:S(2)}) copy-start(f32[31,1280]{1,0:T(8,128)} %copy-done.6) | copy-start | bytes 476164

commit v2 on v1

--- a/solution.py
+++ b/solution.py
@@ -185,14 +185,14 @@
     go_ref, x_ref, pre_ref, q_ref, k_ref, v_ref, counts_ref, gain_ref, kern_ref,
     w_in_ref, w_conv_ref, w_attn_ref,
     resid_ref, qg_ref, kg_ref, vg_ref, taps_ref, gaing_ref,
-    full_conv, full_in, full_attn, glu_ref, gext_ref, halo_ref, seg_ref, segc_ref,
+    full_conv, full_in, full_attn, glu_ref, gext_ref, halo_ref, seg_ref, segc_ref, mask_ref, kt_ref, vt_ref,
     conv_ref, cog_ref, cg_ref, cext_ref, gin_ref, ng_ref, probs_ref, ctx_ref, dout_ref,
-    qa_ref, ka_ref, va_ref, sums_ref, part_a, mine_a, part_b, total_ref,
+    ka_ref, va_ref, sums_ref, part_a, mine_a, part_b, total_ref,
     send_sem, recv_sem, local_sem,
 ):
     f32, bf16 = jnp.float32, jnp.bfloat16
     rows, width = go_ref.shape
-    total, cols = q_ref.shape
+    cols, total = q_ref.shape
     heads = cols // HD
     n_seq = total // rows
     n_dp = 8
@@ -272,6 +272,9 @@
         arrive(piece(m, diag, moff, PART), base + 4)
         push(piece(m, diag, moff, PART), piece(m, diag, moff, PART), base + 8, me, zn)
         arrive(piece(m, diag, 2 * PART, rest), base + 5)
+
+    def forward_sib(m):
+        base = 13 * m
         for k, dev in ((6, xn), (7, yn)):
             arrive(piece(m, dev, toff, PART), base + k)
             push(piece(m, dev, 0, shard), piece(m, dev, 0, shard), base + k + 4, sib, z)
@@ -308,6 +311,7 @@
         dst[rows + 16 : rows + 32, :] = halo_ref[slot + 1].astype(f32)
 
     send_own(0)
+    send_own(1)
 
     @pl.loop(0, width // LANES)
     def _(n):
@@ -324,25 +328,27 @@
         z * rows - 16 + lax.broadcasted_iota(jnp.int32, (rows + 32, LANES), 0)
     )
     segc_ref[...] = segments(lax.broadcasted_iota(jnp.int32, (total, LANES), 0))
+    for o in range(KW):
+        same = seg_ref[o + 1 : o + 1 + rows, :] == seg_ref[16 : 16 + rows, :]
+        mask_ref[o] = jnp.where(same, 1.0, 0.0)
 
     scale = 1.0 / math.sqrt(HD)
     qblock = 256
 
-    def window(h):
-        low = h * HD // LANES * LANES
-        high = min(-(-(h + 1) * HD // LANES) * LANES, cols)
-        lane = low + lax.broadcasted_iota(jnp.int32, (1, high - low), 1)
-        inside = jnp.where((lane >= h * HD) & (lane < (h + 1) * HD), 1.0, 0.0).astype(bf16)
-        return low, high, inside
+    def head(h):
+        return pl.ds(pl.multiple_of(h * HD, 16), HD)
 
     def make_probs(h):
-        low, high, inside = window(h)
+        keys = k_ref[head(h), :].astype(f32).T.astype(bf16)
+        kt_ref[...] = keys
+        vt_ref[h] = v_ref[head(h), :].astype(f32).T.astype(bf16)
 
         @pl.loop(0, total // qblock)
         def _(b):
-            queries = q_ref[tiles(b, qblock), low:high]
             scores = (
-                lax.dot_general(k_ref[:, low:high] * inside, queries, NT, preferred_element_type=f32)
+                lax.dot_general(
+                    kt_ref[...], q_ref[head(h), tiles(b, qblock)], NN, preferred_element_type=f32
+                )
                 * scale
             )
             seg_q = segments(b * qblock + lax.broadcasted_iota(jnp.int32, (1, qblock), 1))
@@ -353,25 +359,34 @@
 
     make_probs(0)
     forward_xy(0)
-    send_own(1)
+    send_own(2)
 
     take_halo(gext_ref, 0, 39)
+    reach = rows // 2 + 24
+
+    def taps(r):
+        return [(o, o + 1 - r) for o in range(KW) if (o + 1) % 8 == r]
 
     @pl.loop(0, width // LANES)
     def _(n):
         c = tiles(n, LANES)
-        seg_own = seg_ref[16 : 16 + rows, :]
-        acc = jnp.zeros((rows, LANES), f32)
-        for o in range(KW):
-            same = seg_ref[o + 1 : o + 1 + rows, :] == seg_own
-            acc = acc + kern_ref[o : o + 1, c] * jnp.where(
-                same, gext_ref[o + 1 : o + 1 + rows, c], 0.0
-            )
-        conv_ref[:, c] = acc
+        for low in (0, rows // 2):
+            acc = jnp.zeros((rows // 2, LANES), f32)
+            for r in range(8):
+                near = gext_ref[low + r : low + r + reach, c]
+                for o, at in taps(r):
+                    here = near[at : at + rows // 2] * mask_ref[o, low : low + rows // 2, :]
+                    acc = acc + kern_ref[o : o + 1, c] * here
+            conv_ref[low : low + rows // 2, c] = acc
 
     forward_diag(0)
-    for h in range(1, heads):
+
+    @pl.loop(1, heads - 1)
+    def _(h):
         make_probs(h)
+
+    forward_sib(0)
+    make_probs(heads - 1)
     finish(0)
 
     @pl.loop(0, width // 256)
@@ -389,29 +404,45 @@
         cext_ref[16 : 16 + rows, c] = grad.astype(f32)
 
     send_halo(cg_ref, 2, 41)
+    take_halo(cext_ref, 2, 41)
+
+    def back(first, last):
+        @pl.loop(first, last)
+        def _(n):
+            c = tiles(n, LANES)
+            c2 = pl.ds(pl.multiple_of(width + n * LANES, LANES), LANES)
+            for low in (0, rows // 2):
+                part = pl.ds(low, rows // 2)
+                grad_own = cext_ref[low + 16 : low + 16 + rows // 2, c]
+                acc = jnp.zeros((rows // 2, LANES), f32)
+                for r in range(8):
+                    near_c = cext_ref[low + r : low + r + reach, c]
+                    near_g = gext_ref[low + r : low + r + reach, c]
+                    for o, at in taps(r):
+                        mask = mask_ref[o, part, :]
+                        acc = acc + kern_ref[KW - 1 - o : KW - o, c] * (
+                            near_c[at : at + rows // 2] * mask
+                        )
+                        pair = grad_own * (near_g[at : at + rows // 2] * mask)
+                        pair = jnp.sum(pair, axis=0, keepdims=True)
+                        if low == 0:
+                            sums_ref[o : o + 1, c] = pair
+                        else:
+                            sums_ref[o : o + 1, c] += pair
+                gate = jax.nn.sigmoid(pre_ref[part, c2].astype(f32))
+                scaled = acc * gate
+                gin_ref[part, c] = scaled.astype(bf16)
+                gin_ref[part, c2] = (scaled * pre_ref[part, c].astype(f32) * (1.0 - gate)).astype(bf16)
+
+    blocks = width // LANES
     forward_xy(1)
-    send_own(2)
-    take_halo(cext_ref, 2, 41)
-
-    @pl.loop(0, width // LANES)
-    def _(n):
-        c = tiles(n, LANES)
-        c2 = pl.ds(pl.multiple_of(width + n * LANES, LANES), LANES)
-        seg_own = seg_ref[16 : 16 + rows, :]
-        grad_own = cext_ref[16 : 16 + rows, c]
-        acc = jnp.zeros((rows, LANES), f32)
-        for o in range(KW):
-            same = seg_ref[o + 1 : o + 1 + rows, :] == seg_own
-            near = jnp.where(same, cext_ref[o + 1 : o + 1 + rows, c], 0.0)
-            acc = acc + kern_ref[KW - 1 - o : KW - o, c] * near
-            pair = jnp.where(same, grad_own * gext_ref[o + 1 : o + 1 + rows, c], 0.0)
-            sums_ref[o : o + 1, c] = jnp.sum(pair, axis=0, keepdims=True)
-        gate = jax.nn.sigmoid(pre_ref[:, c2].astype(f32))
-        scaled = acc * gate
-        gin_ref[:, c] = scaled.astype(bf16)
-        gin_ref[:, c2] = (scaled * pre_ref[:, c].astype(f32) * (1.0 - gate)).astype(bf16)
-
+    back(0, blocks * 2 // 5)
     forward_diag(1)
+    back(blocks * 2 // 5, blocks * 7 // 10)
+    forward_xy(2)
+    back(blocks * 7 // 10, blocks)
+    forward_sib(1)
+    forward_diag(2)
     finish(1)
 
     @pl.loop(0, width // 256)
@@ -419,8 +450,9 @@
         c = tiles(n, 256)
         ng_ref[:, c] = lax.dot_general(gin_ref[...], full_in[c, :], NT, preferred_element_type=f32)
 
-    forward_xy(2)
+    forward_sib(2)
     sums_ref[KW : KW + 1, :] = jnp.zeros((1, width), f32)
+    gain = gain_ref[...].reshape(1, width)
 
     @pl.loop(0, rows // 16)
     def _(n):
@@ -430,7 +462,7 @@
         inv = 1.0 / jnp.sqrt(jnp.mean(centred * centred, axis=1, keepdims=True) + 1e-05)
         normed = centred * inv
         grad = ng_ref[r, :]
-        scaled = grad * gain_ref[...]
+        scaled = grad * gain
         back = inv * (
             scaled
             - jnp.mean(scaled, axis=1, keepdims=True)
@@ -439,7 +471,6 @@
         resid_ref[r, :] = (go_ref[r, :].astype(f32) + back).astype(bf16)
         sums_ref[KW : KW + 1, :] += jnp.sum(grad * normed, axis=0, keepdims=True)
 
-    forward_diag(2)
     for s in range(1, n_seq):
         to = (z + s) % n_seq
         push(sums_ref.at[tiles(to, 8), :], part_a.at[s - 1], 45 + s, me, to)
@@ -448,13 +479,13 @@
     for s in range(1, n_seq + 1):
         to = (z + s) % n_seq
         out = lax.dot_general(
-            resid_ref[...], full_attn[tiles(to, cols), :], NT, preferred_element_type=f32
+            full_attn[tiles(to, cols), :], resid_ref[...], NT, preferred_element_type=f32
         ).astype(bf16)
         if s < n_seq:
             ctx_ref[s - 1] = out
-            push(ctx_ref.at[s - 1], dout_ref.at[tiles(z, rows), :], 42 + s, me, to)
+            push(ctx_ref.at[s - 1], dout_ref.at[z], 42 + s, me, to)
         else:
-            dout_ref[tiles(z, rows), :] = out
+            dout_ref[z] = out
 
     for s in range(1, n_seq):
         arrive(part_a.at[s - 1], 45 + s)
@@ -464,50 +495,51 @@
     part_b[me] = mine_a[...]
 
     for s in range(1, n_seq):
-        arrive(dout_ref.at[tiles((z + n_seq - s) % n_seq, rows), :], 42 + s)
-
-    qa_ref[...] = jnp.zeros((total, cols), f32)
-    ka_ref[...] = jnp.zeros((total, cols), f32)
-    va_ref[...] = jnp.zeros((total, cols), f32)
-    for h in range(heads):
-        low, high, inside = window(h)
-
-        @pl.loop(0, total // qblock)
-        def _(b):
-            r = tiles(b, qblock)
-            probs = probs_ref[h, b]
-            dout = dout_ref[r, low:high] * inside
-            va_ref[:, low:high] += lax.dot_general(
-                probs.astype(bf16), dout, NN, preferred_element_type=f32
-            )
-            prob_grad = lax.dot_general(v_ref[:, low:high], dout, NT, preferred_element_type=f32)
-            delta = jnp.sum(probs * prob_grad, axis=0, keepdims=True)
-            score_grad = (probs * (prob_grad - delta)).astype(bf16)
-            ka_ref[:, low:high] += lax.dot_general(
-                score_grad, q_ref[r, low:high] * inside, NN, preferred_element_type=f32
-            )
-            qa_ref[r, low:high] += lax.dot_general(
-                score_grad, k_ref[:, low:high] * inside, TN, preferred_element_type=f32
-            )
-
-        if h == 1:
-            for s in range(1, n_dp):
-                arrive(part_b.at[(me + n_dp - s) % n_dp], 48 + s)
-            chunk = part_b[0]
-            for i in range(1, n_dp):
-                chunk = chunk + part_b[i]
-            total_ref[tiles(z, 8), :] = chunk
-            for s in range(1, n_seq):
-                block = total_ref.at[tiles(z, 8), :]
-                push(block, block, 55 + s, me, (z + s) % n_seq)
-
-    qg_ref[...] = (qa_ref[...] * scale).astype(bf16)
-    kg_ref[...] = (ka_ref[...] * scale).astype(bf16)
-    vg_ref[...] = va_ref[...].astype(bf16)
+        arrive(dout_ref.at[(z + n_seq - s) % n_seq], 42 + s)
+
+    def attend(first, last):
+        @pl.loop(first, last)
+        def _(h):
+            hd = head(h)
+            per = qblock // rows
+            for b in range(total // qblock):
+                q = pl.ds(b * qblock, qblock)
+                probs = probs_ref[h, b]
+                dout = jnp.concatenate(
+                    [dout_ref[b * per + i, hd, :] for i in range(per)], axis=1
+                )
+                prob_grad = lax.dot_general(vt_ref[h], dout, NN, preferred_element_type=f32)
+                delta = jnp.sum(probs * prob_grad, axis=0, keepdims=True)
+                score_grad = (probs * (prob_grad - delta)).astype(bf16)
+                value_part = lax.dot_general(dout, probs.astype(bf16), NT, preferred_element_type=f32)
+                key_part = lax.dot_general(q_ref[hd, q], score_grad, NT, preferred_element_type=f32)
+                query_part = lax.dot_general(k_ref[hd, :], score_grad, NN, preferred_element_type=f32)
+                qg_ref[hd, q] = (query_part * scale).astype(bf16)
+                if b == 0:
+                    va_ref[...] = value_part
+                    ka_ref[...] = key_part
+                else:
+                    va_ref[...] += value_part
+                    ka_ref[...] += key_part
+            kg_ref[hd, :] = (ka_ref[...] * scale).astype(bf16)
+            vg_ref[hd, :] = va_ref[...].astype(bf16)
+
+    attend(0, heads // 2)
+    for s in range(1, n_dp):
+        arrive(part_b.at[(me + n_dp - s) % n_dp], 48 + s)
+    chunk = part_b[0]
+    for i in range(1, n_dp):
+        chunk = chunk + part_b[i]
+    total_ref[tiles(z, 8), :] = chunk
+    for s in range(1, n_seq):
+        block = total_ref.at[tiles(z, 8), :]
+        push(block, block, 55 + s, me, (z + s) % n_seq)
+    attend(heads // 2, heads)
+
     for s in range(1, n_seq):
         arrive(total_ref.at[tiles((z + n_seq - s) % n_seq, 8), :], 55 + s)
     taps_ref[...] = total_ref[0:KW, :]
-    gaing_ref[...] = total_ref[KW : KW + 1, :]
+    gaing_ref[...] = total_ref[KW : KW + 1, :].reshape(width)
     for copy in sent:
         copy.wait_send()
 
@@ -518,6 +550,7 @@
 ):
     rows, width = grad_out.shape
     total, cols = queries.shape
+    queries, keys, values = queries.T, keys.T, values.T
     heads = cols // HD
     f32, bf16 = jnp.float32, jnp.bfloat16
     vmem = pl.BlockSpec(memory_space=pltpu.VMEM)
@@ -527,11 +560,11 @@
         fused,
         out_shape=(
             jax.ShapeDtypeStruct((rows, width), bf16),
-            jax.ShapeDtypeStruct((total, cols), bf16),
-            jax.ShapeDtypeStruct((total, cols), bf16),
-            jax.ShapeDtypeStruct((total, cols), bf16),
+            jax.ShapeDtypeStruct((cols, total), bf16),
+            jax.ShapeDtypeStruct((cols, total), bf16),
+            jax.ShapeDtypeStruct((cols, total), bf16),
             jax.ShapeDtypeStruct((KW, width), f32),
-            jax.ShapeDtypeStruct((1, width), f32),
+            jax.ShapeDtypeStruct((width,), f32),
         ),
         in_specs=[vmem] * 6 + [smem] + [vmem] * 2 + [hbm] * 3,
         out_specs=(vmem,) * 6,
@@ -544,6 +577,9 @@
             pltpu.VMEM((4, 16, width), bf16),
             pltpu.VMEM((rows + 32, LANES), jnp.int32),
             pltpu.VMEM((total, LANES), jnp.int32),
+            pltpu.VMEM((KW, rows, LANES), f32),
+            pltpu.VMEM((total, HD), bf16),
+            pltpu.VMEM((heads, total, HD), bf16),
             pltpu.VMEM((rows, width), f32),
             pltpu.VMEM((rows, width), f32),
             pltpu.VMEM((rows, width), bf16),
@@ -551,11 +587,10 @@
             pltpu.VMEM((rows, 2 * width), bf16),
             pltpu.VMEM((rows, width), f32),
             pltpu.VMEM((heads, total // 256, total, 256), f32),
-            pltpu.VMEM((3, rows, cols), bf16),
-            pltpu.VMEM((total, cols), bf16),
-            pltpu.VMEM((total, cols), f32),
-            pltpu.VMEM((total, cols), f32),
-            pltpu.VMEM((total, cols), f32),
+            pltpu.VMEM((3, cols, rows), bf16),
+            pltpu.VMEM((4, cols, rows), bf16),
+            pltpu.VMEM((HD, total), f32),
+            pltpu.VMEM((HD, total), f32),
             pltpu.VMEM((KW + 1, width), f32),
             pltpu.VMEM((3, 8, width), f32),
             pltpu.VMEM((8, width), f32),
@@ -570,9 +605,9 @@
         ),
     )(
         grad_out, saved_input, pre_glu, queries, keys, values, frame_counts,
-        norm_gain.reshape(1, width), kernel, w_in, w_conv_out, w_attn_out,
+        norm_gain, kernel, w_in, w_conv_out, w_attn_out,
     )
-    return outs[:5] + (outs[5].reshape(width),)
+    return (outs[0], outs[1].T, outs[2].T, outs[3].T, outs[4], outs[5])
 
 
 def solution(mesh):

time: 97.5 us -> 104 us (1.067)
  local copies, waits for them, and re-layouts: 9.97 us -> 13.3 us
  Pallas kernels: 85.9 us -> 89.1 us
    unnamed x30 -> x26, local copies, waits for them, and re-layouts: 9.27 us -> 13.3 us
    pallas_call x1, Pallas kernels: 85.9 us -> 89.1 us  [fused_local(): pl.pallas_call(fused, out_shape=(jax.ShapeDtypeStruct((rows, width), bf16...]
where the time goes in v2:
time: 104 us; the launch traced here: 103 us
  Pallas kernels  89.1 us (86%)
  local copies, waits for them, and re-layouts  13.3 us (13%)
    pallas_call x1, Pallas kernels, fused_local(): pl.pallas_call(fused, out_shape=(jax.ShapeDtypeStruct((rows, width), bf16...  89.1 us
    unnamed x26, local copies, waits for them, and re-layouts  13.3 us

profile of v2, /device:TPU:0, one launch (start us, length us, event | category | flops | bytes accessed | tf_op | source)
XLA Modules:
  0.0 103.0 jit_solution(426462831503470062)
XLA Ops:
  0.6 0.0 copy-start.9
  0.6 0.6 copy-done.9
  1.3 0.0 copy-start
  1.3 1.0 copy-done
  2.3 0.0 copy-start.1
  2.3 1.0 copy-done.1
  3.3 0.0 copy-start.2
  3.3 1.0 copy-done.2
  4.3 0.0 copy-start.3
  4.3 1.0 copy-done.3
  5.2 0.0 copy-start.4
  5.2 1.0 copy-done.4
  6.2 0.0 copy-start.5
  6.2 1.0 copy-done.5
  7.2 0.0 copy-start.6
  7.2 1.0 copy-done.6
  8.2 0.0 copy-start.7
  8.2 0.9 copy-done.7
  9.1 0.0 copy-start.8
  9.1 0.7 copy-done.8
  9.8 89.1 %shard_map.163 = (bf16[128,1280]{1,0:T(8,128)(2,1)S(1)}, bf16[320,512]{1,0:T(8,128)(2,1)S(1)}, bf16[320,512]{1,0:T(8,128)(2,1)S(1)}, bf16[320,512]{1,0:T(8,128)(...) custom-call(bf16[128,1280]{1,0:T(8,128)(2,1)S(1)} %copy-done.2, bf16[128,1280]{1,0:T(8,128)(2,1)S(1)} %copy-done.3, ...), custom_call_target="tpu_custom_call" | custom-call | tf_op jit(solution)/shard_map/pallas_call | solution.py:559
  98.9 0.7 copy.24
  99.6 0.7 copy.25
  100.3 0.7 copy.26
  101.0 0.7 copy.27
  101.8 0.7 copy.28
  102.4 0.6 copy.29
Async XLA Ops:
  0.6 0.7 copy-start.9
  1.3 1.0 copy-start
  2.3 1.0 copy-start.1
  3.3 1.0 copy-start.2
  4.3 1.0 copy-start.3
  5.2 1.0 copy-start.4
  6.2 1.0 copy-start.5
  7.2 1.0 copy-start.6
  8.2 0.9 copy-start.7
  9.1 0.7 copy-start.8

commit v3 on v2

--- a/solution.py
+++ b/solution.py
@@ -182,12 +182,13 @@
 
 
 def fused(
-    go_ref, x_ref, pre_ref, q_ref, k_ref, v_ref, counts_ref, gain_ref, kern_ref,
+    go_hbm, x_hbm, pre_hbm, q_hbm, k_hbm, v_hbm, counts_ref, gain_hbm, kern_hbm,
     w_in_ref, w_conv_ref, w_attn_ref,
     resid_ref, qg_ref, kg_ref, vg_ref, taps_ref, gaing_ref,
     full_conv, full_in, full_attn, glu_ref, gext_ref, halo_ref, seg_ref, segc_ref, mask_ref, kt_ref, vt_ref,
     conv_ref, cog_ref, cg_ref, cext_ref, gin_ref, ng_ref, probs_ref, ctx_ref, dout_ref,
     ka_ref, va_ref, sums_ref, part_a, mine_a, part_b, total_ref,
+    go_ref, x_ref, pre_ref, q_ref, k_ref, v_ref, gain_ref, kern_ref,
     send_sem, recv_sem, local_sem,
 ):
     f32, bf16 = jnp.float32, jnp.bfloat16
@@ -209,6 +210,16 @@
     moff = PART * (z % 2)
     toff = PART - moff
 
+    loads = [
+        pltpu.make_async_copy(source, target, local_sem.at[3 + i])
+        for i, (source, target) in enumerate((
+            (pre_hbm, pre_ref), (k_hbm, k_ref), (q_hbm, q_ref), (v_hbm, v_ref),
+            (kern_hbm, kern_ref), (go_hbm, go_ref), (x_hbm, x_ref), (gain_hbm, gain_ref),
+        ))
+    ]
+    for load in loads:
+        load.start()
+
     barrier = pltpu.get_barrier_semaphore()
     for s in range(1, n_dp):
         pl.semaphore_signal(barrier, inc=1, device_id=((me + s) % n_dp, z), device_id_type=MESH)
@@ -311,7 +322,7 @@
         dst[rows + 16 : rows + 32, :] = halo_ref[slot + 1].astype(f32)
 
     send_own(0)
-    send_own(1)
+    loads[0].wait()
 
     @pl.loop(0, width // LANES)
     def _(n):
@@ -357,9 +368,11 @@
             expd = jnp.exp(scores - jnp.max(scores, axis=0, keepdims=True))
             probs_ref[h, b] = expd * (1.0 / jnp.sum(expd, axis=0, keepdims=True))
 
+    for load in loads[1:]:
+        load.wait()
     make_probs(0)
     forward_xy(0)
-    send_own(2)
+    send_own(1)
 
     take_halo(gext_ref, 0, 39)
     reach = rows // 2 + 24
@@ -436,6 +449,7 @@
 
     blocks = width // LANES
     forward_xy(1)
+    send_own(2)
     back(0, blocks * 2 // 5)
     forward_diag(1)
     back(blocks * 2 // 5, blocks * 7 // 10)
@@ -544,6 +558,17 @@
         copy.wait_send()
 
 
+def store_all(*refs):
+    sources, targets, sems = refs[:6], refs[6:12], refs[12]
+    copies = [
+        pltpu.make_async_copy(sources[i], targets[i], sems.at[i]) for i in range(6)
+    ]
+    for copy in copies:
+        copy.start()
+    for copy in copies:
+        copy.wait()
+
+
 def fused_local(
     grad_out, saved_input, pre_glu, queries, keys, values, frame_counts, norm_gain, kernel,
     w_in, w_conv_out, w_attn_out,
@@ -555,7 +580,7 @@
     f32, bf16 = jnp.float32, jnp.bfloat16
     vmem = pl.BlockSpec(memory_space=pltpu.VMEM)
     smem = pl.BlockSpec(memory_space=pltpu.SMEM)
-    hbm = pl.BlockSpec(memory_space=pl.ANY)
+    hbm = pl.BlockSpec(memory_space=pltpu.HBM)
     outs = pl.pallas_call(
         fused,
         out_shape=(
@@ -566,7 +591,7 @@
             jax.ShapeDtypeStruct((KW, width), f32),
             jax.ShapeDtypeStruct((width,), f32),
         ),
-        in_specs=[vmem] * 6 + [smem] + [vmem] * 2 + [hbm] * 3,
+        in_specs=[hbm] * 6 + [smem] + [hbm] * 5,
         out_specs=(vmem,) * 6,
         scratch_shapes=[
             pltpu.VMEM((width, width), bf16),
@@ -596,17 +621,33 @@
             pltpu.VMEM((8, width), f32),
             pltpu.VMEM((8, 8, width), f32),
             pltpu.VMEM((KW + 1, width), f32),
+            pltpu.VMEM((rows, width), bf16),
+            pltpu.VMEM((rows, width), bf16),
+            pltpu.VMEM((rows, 2 * width), bf16),
+            pltpu.VMEM((cols, total), bf16),
+            pltpu.VMEM((cols, total), bf16),
+            pltpu.VMEM((cols, total), bf16),
+            pltpu.VMEM((width,), f32),
+            pltpu.VMEM((KW, width), f32),
             pltpu.SemaphoreType.DMA((COPIES,)),
             pltpu.SemaphoreType.DMA((COPIES,)),
-            pltpu.SemaphoreType.DMA((3,)),
+            pltpu.SemaphoreType.DMA((11,)),
         ],
         compiler_params=pltpu.CompilerParams(
-            collective_id=0, has_side_effects=True, vmem_limit_bytes=50 * 1024 * 1024
+            collective_id=0, has_side_effects=True, vmem_limit_bytes=63 * 1024 * 1024
         ),
     )(
         grad_out, saved_input, pre_glu, queries, keys, values, frame_counts,
         norm_gain, kernel, w_in, w_conv_out, w_attn_out,
     )
+    outs = pl.pallas_call(
+        store_all,
+        out_shape=tuple(jax.ShapeDtypeStruct(o.shape, o.dtype) for o in outs),
+        in_specs=[hbm] * 6,
+        out_specs=(hbm,) * 6,
+        scratch_shapes=[pltpu.SemaphoreType.DMA((6,))],
+        compiler_params=pltpu.CompilerParams(vmem_limit_bytes=63 * 1024 * 1024),
+    )(*outs)
     return (outs[0], outs[1].T, outs[2].T, outs[3].T, outs[4], outs[5])
 
 

time: 104 us -> 127 us (1.22)
  Pallas kernels: 89.1 us -> 127 us
  local copies, waits for them, and re-layouts: 13.3 us -> 0 us
    pallas_call x0 -> x1, Pallas kernels: none -> 46 us  [fused_local(): pl.pallas_call(store_all, out_shape=tuple((jax.ShapeDtypeStruct(o.shape,...]
    unnamed x26 -> x0, local copies, waits for them, and re-layouts: 13.3 us -> none
    pallas_call x1, Pallas kernels: 89.1 us -> 80.6 us  [fused_local(): pl.pallas_call(fused, out_shape=(jax.ShapeDtypeStruct((rows, width), bf16...]
where the time goes in v3:
time: 127 us
  Pallas kernels  127 us (100%)
    pallas_call x1, Pallas kernels, fused_local(): pl.pallas_call(fused, out_shape=(jax.ShapeDtypeStruct((rows, width), bf16...  80.6 us
    pallas_call x1, Pallas kernels, fused_local(): pl.pallas_call(store_all, out_shape=tuple((jax.ShapeDtypeStruct(o.shape,...  46 us

profile of v3, /device:TPU:0, one launch (start us, length us, event | category | flops | bytes accessed | tf_op | source)
XLA Modules:
  0.0 127.2 jit_solution(14971812171712327883)
XLA Ops:
  0.6 80.6 %shard_map.163 = (bf16[128,1280]{1,0:T(8,128)(2,1)}, bf16[320,512]{1,0:T(8,128)(2,1)}, bf16[320,512]{1,0:T(8,128)(2,1)}, bf16[320,512]{1,0:T(8,128)(2,1)}, f32[31,1280]{1,0:T(8,128)}, /*index=5*/f32[1280]{0:T(1024)}) custom-call(bf16[128,1280]{1,0:T(8,128)(2,1)} %go_hbm.1, bf16[128,1280]{1,0:T(8,128)(2,1)} %x_hbm.1, bf16[128,2560]{1,0:T(8,128)(2,1)} %pre_hbm.1, ...), custom_call_target="tpu_custom_call" | custom-call | tf_op jit(solution)/shard_map/pallas_call | solution.py:584
  81.2 46.0 %shard_map.164 = (bf16[128,1280]{1,0:T(8,128)(2,1)}, bf16[320,512]{1,0:T(8,128)(2,1)}, bf16[320,512]{1,0:T(8,128)(2,1)}, bf16[320,512]{1,0:T(8,128)(2,1)}, f32[31,1280]{1,0:T(8,128)}, /*index=5*/f32[1280]{0:T(1024)}) custom-call(bf16[128,1280]{1,0:T(8,128)(2,1)} %get-tuple-element.18.refs_0_, bf16[320,512]{1,0:T(8,128)(2,1)} %get-tuple-element.19.refs_1_, ...), custom_call_target="tpu_custom_call" | custom-call | tf_op jit(solution)/shard_map/pallas_call | solution.py:643
